TPU v7x, 32 devices: a whole 2x2x4 slice. The times are simulated.
32 devices in a mesh: gx: 4 (over z), gy: 8 (over y, x, core).
Axes of the slice: x: 2, y: 2, z: 4, core: 2. Of those that a mesh axis runs over, the one named last changes fastest.
Arguments:
- seismic: float32 [512, 512, 256], P('gx', 'gy'), may hold values from -41 to 41, as said below
Outputs:
- shift_field: float32 [512, 512, 256], P('gx', 'gy')
- residual: float32 [512, 512, 256], P('gx', 'gy')
Inputs may be any that keep to these rules, and one draw needn't show every extreme that they name: `seismic`: recorded amplitudes of the window.
All inputs are finite; a program needn't handle non-finite values.
Results may differ from a plain program's by a relative error of at most 0.0003.
Values sent between devices are 32-bit elements; how exact they have to be, the bound alone decides.
A program may use at most 320 MiB of HBM per device.

v0:
```python
import jax
import jax.numpy as jnp
from jax import lax
from jax.sharding import PartitionSpec as P

NX = 512
NY = 512
ITERS = 2
damping = 0.001
floor_term = 0.5
highest = lax.Precision.HIGHEST


def extended(block, sides, width):
    for axis, dim in sides:
        count = lax.axis_size(axis)
        forward = [(i, i + 1) for i in range(count - 1)]
        backward = [(target, source) for source, target in forward]
        low = lax.ppermute(
            lax.slice_in_dim(block, block.shape[dim] - width, None, axis=dim), axis, forward
        )
        high = lax.ppermute(lax.slice_in_dim(block, 0, width, axis=dim), axis, backward)
        block = jnp.concatenate([low, block, high], axis=dim)
    return block


def cut(field, start, stop, axis):
    return lax.slice_in_dim(field, start, stop, axis=axis)


def smooth_axis(field, axis):
    length = field.shape[axis]
    return 0.25 * (
        cut(field, 0, length - 2, axis)
        + 2.0 * cut(field, 1, length - 1, axis)
        + cut(field, 2, length, axis)
    )


def pad_time(field):
    return jnp.pad(field, ((0, 0), (0, 0), (1, 1)))


def smooth_all(field):
    return smooth_axis(pad_time(smooth_axis(smooth_axis(field, 0), 1)), 2)


def tensor_fields(padded, inside_x, inside_y):
    mask = inside_x[:, None, None] * inside_y[None, :, None]
    grad_x = 0.5 * (padded[2:, 1:-1] - padded[:-2, 1:-1]) * mask
    grad_y = 0.5 * (padded[1:-1, 2:] - padded[1:-1, :-2]) * mask
    timed = pad_time(padded[1:-1, 1:-1])
    grad_t = 0.5 * (timed[:, :, 2:] - timed[:, :, :-2]) * mask
    cross_x = smooth_all(grad_x * grad_t)
    cross_y = smooth_all(grad_y * grad_t)
    along_t = smooth_all(grad_t * grad_t) + floor_term
    spread = smooth_all(grad_x * grad_x + grad_y * grad_y)
    return (-cross_x / along_t, -cross_y / along_t, along_t / (along_t + spread))


def cosine_table(order):
    freq = jnp.arange(order, dtype=jnp.float32)[:, None]
    place = jnp.arange(order, dtype=jnp.float32)[None, :]
    scale = jnp.where(freq == 0.0, jnp.sqrt(1.0 / order), jnp.sqrt(2.0 / order)).astype(jnp.float32)
    return scale * jnp.cos(jnp.pi * (place + 0.5) * freq / order)


def eigen_values(order):
    freq = jnp.arange(order, dtype=jnp.float32)
    return 2.0 - 2.0 * jnp.cos(jnp.pi * freq / order)


def combine_terms(field, upper_x, lower_x, upper_y, lower_y, weight_x, weight_y, prior_x, prior_y):
    return (
        damping * field
        + weight_x * (field - upper_x)
        + prior_x * (field - lower_x)
        + weight_y * (field - upper_y)
        + prior_y * (field - lower_y)
    )


def operate(field, weight_x, weight_y, prior_x, prior_y):
    padded = extended(field, (("gx", 0), ("gy", 1)), 1)
    return combine_terms(
        field,
        padded[2:, 1:-1],
        padded[:-2, 1:-1],
        padded[1:-1, 2:],
        padded[1:-1, :-2],
        weight_x,
        weight_y,
        prior_x,
        prior_y,
    )


def solve_front(front, table_x, table_y, plane_denom):
    hat = jnp.einsum("ki,tij->tkj", table_x, front, precision=highest)
    hat = jnp.einsum("lj,tkj->tkl", table_y, hat, precision=highest)
    hat = hat / plane_denom
    hat = jnp.einsum("lj,tkl->tkj", table_y, hat, precision=highest)
    return jnp.einsum("ki,tkj->tij", table_x, hat, precision=highest)


def slice_solve(whole, table_x, table_y, plane_denom):
    front = jnp.transpose(whole, (2, 0, 1))
    return jnp.transpose(solve_front(front, table_x, table_y, plane_denom), (1, 2, 0))


def reorder_back(back, rows_x, rows_y, parts_x, parts_y, depth):
    per = depth // (parts_x * parts_y)
    target = jnp.arange(depth, dtype=jnp.int32)
    outer = target // (parts_y * per)
    middle = target // per % parts_y
    source = middle * (parts_x * per) + outer * per + target % per
    select = (jnp.arange(depth, dtype=jnp.int32)[:, None] == source[None, :]).astype(jnp.float32)
    flat = back.reshape(rows_x * rows_y, depth)
    return jnp.dot(flat, select, precision=highest, preferred_element_type=jnp.float32).reshape(
        rows_x, rows_y, depth
    )


def inner(first, second):
    return lax.psum(jnp.sum(first * second), ("gx", "gy"))


def solve(rhs, apply_op, precondition):
    shift_field = jnp.zeros_like(rhs)
    residual = rhs
    precond = precondition(residual)
    direction = precond
    norm_now = inner(residual, precond)
    for step in range(ITERS):
        image = apply_op(direction)
        alpha = norm_now / lax.psum(jnp.sum(direction * image), ("gx", "gy"))
        shift_field = shift_field + alpha * direction
        residual = residual - alpha * image
        if step + 1 < ITERS:
            precond = precondition(residual)
            norm_next = inner(residual, precond)
            direction = precond + norm_next / norm_now * direction
            norm_now = norm_next
    return (shift_field, residual)


def per_device(seismic):
    rows_x, rows_y, depth = seismic.shape
    parts_x = lax.axis_size("gx")
    parts_y = lax.axis_size("gy")
    base_x = lax.axis_index("gx") * rows_x
    base_y = lax.axis_index("gy") * rows_y
    table_x = cosine_table(NX)
    table_y = cosine_table(NY)
    eigen_x = eigen_values(NX)
    eigen_y = eigen_values(NY)
    plane_denom = damping + eigen_x[:, None] + eigen_y[None, :]
    padded = extended(seismic, (("gx", 0), ("gy", 1)), 3)
    grid_x = base_x + jnp.arange(-2, rows_x + 2, dtype=jnp.int32)
    grid_y = base_y + jnp.arange(-2, rows_y + 2, dtype=jnp.int32)
    inside_x = ((grid_x >= 0) & (grid_x < NX)).astype(jnp.float32)
    inside_y = ((grid_y >= 0) & (grid_y < NY)).astype(jnp.float32)
    dip_x, dip_y, weight = tensor_fields(padded, inside_x, inside_y)
    edge_x = grid_x[1:-1]
    edge_y = grid_y[1:-1]
    keep_x = ((edge_x >= 0) & (edge_x < NX - 1)).astype(jnp.float32)
    keep_y = ((edge_y >= 0) & (edge_y < NY - 1)).astype(jnp.float32)
    weight_x = weight * keep_x[:, None, None]
    weight_y = weight * keep_y[None, :, None]
    flux_x = weight_x * dip_x
    flux_y = weight_y * dip_y
    rhs = flux_x[:-2, 1:-1] - flux_x[1:-1, 1:-1] + (flux_y[1:-1, :-2] - flux_y[1:-1, 1:-1])
    own_x = weight_x[1:-1, 1:-1]
    prior_x = weight_x[:-2, 1:-1]
    own_y = weight_y[1:-1, 1:-1]
    prior_y = weight_y[1:-1, :-2]

    def precondition(field):
        whole = lax.all_to_all(
            lax.all_to_all(field, "gx", split_axis=2, concat_axis=0, tiled=True),
            "gy",
            split_axis=2,
            concat_axis=1,
            tiled=True,
        )
        hat = slice_solve(whole, table_x, table_y, plane_denom)
        back = lax.all_to_all(
            lax.all_to_all(hat, "gx", split_axis=0, concat_axis=2, tiled=True),
            "gy",
            split_axis=1,
            concat_axis=2,
            tiled=True,
        )
        return reorder_back(back, rows_x, rows_y, parts_x, parts_y, depth)

    def apply_tiles(field):
        return operate(field, own_x, own_y, prior_x, prior_y)

    return solve(rhs, apply_tiles, precondition)


def solution(mesh):
    placed = (P("gx", "gy", None),)
    return jax.shard_map(
        per_device,
        mesh=mesh,
        in_specs=placed,
        out_specs=(P("gx", "gy", None), P("gx", "gy", None)),
        check_vma=False,
    )
```

profile of v0, /device:TPU:0, one launch (start us, length us, event | category | flops | bytes accessed | tf_op | source)
XLA Modules:
  0.0 2077.2 jit_solution(1720866723027973175)
XLA Ops:
  47.0 54.0 %fusion.77 = (f32[132,68,256]{2,0,1:T(8,128)}, f32[132,68,256]{2,0,1:T(8,128)}, f32[132,68,256]{2,0,1:T(8,128)}, f32[132,68,256]{2,0,1:T(8,128)}) fusion(f32[132,68]{0,1:T(8,128)S(1)} %multiply_multiply_fusion, f32[134,70,256]{2,0,1:T(8,128)} %copy-done.2, f32[132,68,256]{2,0,1:T(8,128)} %slice.298), kind=kLoop, calls=%fused_computation.146 | loop fusion | flops 36765696 | bytes 82758720 | tf_op jit(solution)/shard_map/mul | solution.py:55
  101.0 29.4 %fusion.6 = (f32[130,68,256]{2,0,1:T(8,128)}, f32[130,68,256]{2,0,1:T(8,128)}) fusion(f32[132,68,256]{2,0,1:T(8,128)} %get-tuple-element.29, f32[132,68,256]{2,0,1:T(8,128)} %get-tuple-element.30), kind=kLoop, calls=%fused_computation.23 | loop fusion | flops 18104320 | bytes 72417280 | tf_op jit(solution)/shard_map/mul | solution.py:33
  150.2 29.4 %fusion.2 = (f32[130,68,256]{2,0,1:T(8,128)}, f32[130,68,256]{2,0,1:T(8,128)}) fusion(f32[132,68,256]{2,0,1:T(8,128)} %get-tuple-element.27, f32[132,68,256]{2,0,1:T(8,128)} %get-tuple-element.28), kind=kLoop, calls=%fused_computation.15 | loop fusion | flops 18104320 | bytes 72417280 | tf_op jit(solution)/shard_map/mul | solution.py:33
  203.3 45.0 %fusion.24 = (f32[130,66,256]{2,0,1:T(8,128)}, f32[130,66,256]{2,0,1:T(8,128)}, f32[130,66,256]{2,0,1:T(8,128)}, f32[130,66,256]{2,0,1:T(8,128)}) fusion(f32[130,66,256]{2,0,1:T(8,128)} %broadcast_multiply_fusion.3, f32[130,68,256]{2,0,1:T(8,128)} %get-tuple-element.46, f32[130]{0:T(256)S(1)} %and_convert_fusion.1, f32[130,68,256]{2,0,1:T(8,128)S(1)} %bitcast.93, ...), kind=kLoop, calls=%fused_computation.47 | loop fusion | flops 61501440 | bytes 140575232 | tf_op jit(solution)/shard_map/mul | solution.py:170
  248.3 26.7 %fusion.30 = (f32[130,66,256]{2,0,1:T(8,128)}, f32[130,66,256]{2,0,1:T(8,128)}) fusion(f32[130,66,256]{2,0,1:T(8,128)} %get-tuple-element.24, f32[130,66,256]{2,0,1:T(8,128)} %broadcast_multiply_fusion.2, f32[130,68,256]{2,0,1:T(8,128)} %get-tuple-element.45, f32[130,66,256]{2,0,1:T(8,128)} %get-tuple-element.23, f32[66]{0:T(128)S(1)} %copy-done.9), kind=kLoop, calls=%fused_computation.53 | loop fusion | flops 24161280 | bytes 70287624 | tf_op jit(solution)/shard_map/mul | solution.py:171
  300.0 185.5 %all_to_all.138 = f32[128,64,256]{0,1,2:T(8,128)S(1)} all-to-all(f32[128,64,256]{0,1,2:T(8,128)} %copy.198), channel_id=1, replica_groups=mesh['gx'=4,'gy'=8] {'gx'}, dimensions={2} | all-to-all | bytes 16777216 | tf_op jit(solution)/shard_map/all_to_all | solution.py:180
  501.6 94.0 %all-to-all-done.1 = f32[512,64,64]{0,1,2:T(8,128)} async-done(((f32[512,64,64]{0,1,2:T(8,128)}), f32[512,64,64]{0,1,2:T(8,128)}, u32[]{:S(2)}, u32[]{:S(2)}) %all-to-all-start.1) | async-done | bytes 8388640 | tf_op jit(solution)/shard_map/all_to_all | solution.py:179
  603.7 22.6 %fusion.66 = f32[8,512,512]{2,1,0:T(8,128)S(1)} fusion(f32[512,512,8]{0,2,1:T(8,128)S(1)} %bitcast.102, f32[512]{0:T(512)S(1)} %get-tuple-element.49, f32[512]{0:T(512)S(1)} %get-tuple-element.50), kind=kOutput, calls=%fused_computation.117 | convolution fusion | flops 12885688320 | bytes 16781312 | tf_op jit(solution)/shard_map/ki,tij->tkj/dot_general | solution.py:99
  626.3 34.1 %fusion.64 = f32[8,512,512]{2,1,0:T(8,128)S(1)} fusion(f32[8,512,512]{2,1,0:T(8,128)S(1)} %fusion.66, f32[512]{0:T(512)S(1)} %get-tuple-element.49, f32[512]{0:T(512)S(1)} %get-tuple-element.50), kind=kOutput, calls=%fused_computation.115 | convolution fusion | flops 12885688320 | bytes 16781312 | tf_op jit(solution)/shard_map/lj,tkj->tkl/dot_general | solution.py:100
  680.2 23.2 %convolution_bitcast_fusion.1 = f32[512,512,8]{0,1,2:T(8,128)} fusion(f32[8,512,512]{1,2,0:T(8,128)S(1)} %fusion.72, f32[512]{0:T(512)S(1)} %get-tuple-element.49, f32[512]{0:T(512)S(1)} %get-tuple-element.50), kind=kOutput, calls=%fused_computation.144 | convolution fusion | flops 12885688320 | bytes 16781312 | tf_op jit(solution)/shard_map/ki,tkj->tij/dot_general | solution.py:103
  713.9 184.9 %all_to_all.139 = f32[512,512,8]{1,2,0:T(8,128)S(1)} all-to-all(f32[512,512,8]{1,2,0:T(8,128)} %copy.207), channel_id=1, replica_groups=mesh['gx'=4,'gy'=8] {'gx'}, dimensions={0} | all-to-all | bytes 16777216 | tf_op jit(solution)/shard_map/all_to_all | solution.py:188
  919.2 94.1 %all-to-all-done.3 = f32[128,512,32]{0,2,1:T(8,128)} async-done(((f32[128,512,32]{0,2,1:T(8,128)}), f32[128,512,32]{0,2,1:T(8,128)}, u32[]{:S(2)}, u32[]{:S(2)}) %all-to-all-start.3) | async-done | bytes 8388640 | tf_op jit(solution)/shard_map/all_to_all | solution.py:187
  1069.4 36.8 %multiply_reduce_fusion.2 = (f32[]{:T(128)}, f32[]{:T(128)}, f32[128,64,256]{2,0,1:T(8,128)}) fusion(f32[128,64,256]{2,1,0:T(8,128)} %bitcast.97, f32[128,64,256]{2,0,1:T(8,128)} %fusion.59, f32[128,64,256]{2,0,1:T(8,128)} %copy-done.7, f32[1,64,256]{2,0,1:T(1,128)S(1)} %copy.214, f32[1,64,256]{2,0,1:T(1,128)S(1)} %copy.216, ...), kind=kLoop, calls=%fused_computation.131 | loop fusion | flops 52428800 | bytes 67506184 | tf_op jit(solution)/shard_map/reduce_sum | solution.py:136
  1106.2 41.2 %all-reduce.5 = (f32[]{:T(128)}, f32[]{:T(128)}) all-reduce(f32[]{:T(128)} %get-tuple-element.15, f32[]{:T(128)} %get-tuple-element.14), channel_id=1, replica_groups=mesh['gx'=4,'gy'=8] {'gx','gy'}, use_global_device_ids=true, to_apply=%region_1.2 | all-reduce | flops 2 | bytes 16 | tf_op jit(solution)/shard_map/psum | solution.py:125
  1169.1 186.9 %all_to_all.140 = f32[128,64,256]{0,1,2:T(8,128)S(1)} all-to-all(f32[128,64,256]{0,1,2:T(8,128)} %copy.226), channel_id=1, replica_groups=mesh['gx'=4,'gy'=8] {'gx'}, dimensions={2} | all-to-all | bytes 16777216 | tf_op jit(solution)/shard_map/all_to_all | solution.py:180
  1357.0 97.9 %all_to_all.141 = f32[512,64,64]{0,1,2:T(8,128)} all-to-all(f32[512,64,64]{0,1,2:T(8,128)S(1)} %bitcast.109), channel_id=1, replica_groups=mesh['gx'=4,'gy'=8] {'gy'}, dimensions={2} | all-to-all | bytes 16777216 | tf_op jit(solution)/shard_map/all_to_all | solution.py:179
  1463.1 22.6 %fusion.62 = f32[8,512,512]{2,1,0:T(8,128)S(1)} fusion(f32[512,512,8]{0,2,1:T(8,128)S(1)} %bitcast.103, f32[512]{0:T(512)S(1)} %get-tuple-element.49, f32[512]{0:T(512)S(1)} %get-tuple-element.50), kind=kOutput, calls=%fused_computation.113 | convolution fusion | flops 12885688320 | bytes 16781312 | tf_op jit(solution)/shard_map/ki,tij->tkj/dot_general | solution.py:99
  1485.7 34.1 %fusion.60 = f32[8,512,512]{2,1,0:T(8,128)S(1)} fusion(f32[8,512,512]{2,1,0:T(8,128)S(1)} %fusion.62, f32[512]{0:T(512)S(1)} %get-tuple-element.49, f32[512]{0:T(512)S(1)} %get-tuple-element.50), kind=kOutput, calls=%fused_computation.111 | convolution fusion | flops 12885688320 | bytes 16781312 | tf_op jit(solution)/shard_map/lj,tkj->tkl/dot_general | solution.py:100
  1539.6 23.2 %convolution_bitcast_fusion = f32[512,512,8]{0,1,2:T(8,128)} fusion(f32[8,512,512]{1,2,0:T(8,128)S(1)} %fusion.70, f32[512]{0:T(512)S(1)} %get-tuple-element.49, f32[512]{0:T(512)S(1)} %get-tuple-element.50), kind=kOutput, calls=%fused_computation.143 | convolution fusion | flops 12885688320 | bytes 16781312 | tf_op jit(solution)/shard_map/ki,tkj->tij/dot_general | solution.py:103
  1573.3 187.0 %all_to_all.142 = f32[512,512,8]{1,2,0:T(8,128)S(1)} all-to-all(f32[512,512,8]{1,2,0:T(8,128)} %copy.235), channel_id=1, replica_groups=mesh['gx'=4,'gy'=8] {'gx'}, dimensions={0} | all-to-all | bytes 16777216 | tf_op jit(solution)/shard_map/all_to_all | solution.py:188
  1775.5 97.8 %all_to_all.143 = f32[128,512,32]{0,2,1:T(8,128)S(1)} all-to-all(f32[128,512,32]{0,2,1:T(8,128)} %copy.237), channel_id=1, replica_groups=mesh['gx'=4,'gy'=8] {'gy'}, dimensions={1} | all-to-all | bytes 16777216 | tf_op jit(solution)/shard_map/all_to_all | solution.py:187
  1894.3 38.5 %psum.30 = f32[]{:T(128)} all-reduce(f32[]{:T(128)} %get-tuple-element.43), channel_id=1, replica_groups=mesh['gx'=4,'gy'=8] {'gx','gy'}, use_global_device_ids=true, to_apply=%region_5.6 | all-reduce | flops 1 | bytes 8 | tf_op jit(solution)/shard_map/psum | solution.py:125
  1964.1 20.2 multiply_reduce_fusion
  1984.3 45.3 %psum.31 = f32[]{:T(128)} all-reduce(f32[]{:T(128)} %get-tuple-element.18), channel_id=1, replica_groups=mesh['gx'=4,'gy'=8] {'gx','gy'}, use_global_device_ids=true, to_apply=%region_7.8 | all-reduce | flops 1 | bytes 8 | tf_op jit(solution)/shard_map/psum | solution.py:136
  (118 shorter events, 417.7 us)
Async XLA Ops:
  12.4 10.5 collective-permute-start
  17.3 9.7 collective-permute-start.1
  18.7 16.2 copy-start.6
  28.2 3.8 collective-permute-start.2
  29.5 5.4 collective-permute-start.3
  130.3 14.9 copy-start
  179.6 14.9 copy-start.1
  179.6 20.3 slice-start
  179.6 20.3 slice-start.1
  179.6 21.7 %slice-start.3 = ((s8[9469952]{0:T(1024)(128)(4,1)}), s8[4194304]{0:T(1024)(128)(4,1)S(1)}, s32[]{:S(2)}) async-start(s8[9469952]{0:T(1024)(128)(4,1)} %bitcast.94), calls=%async_computation.11 | async-start | bytes 8388608
  179.6 22.9 %slice-start.4 = ((s8[9469952]{0:T(1024)(128)(4,1)}), s8[4194304]{0:T(1024)(128)(4,1)S(1)}, s32[]{:S(2)}) async-start(s8[9469952]{0:T(1024)(128)(4,1)} %bitcast.94), calls=%async_computation.12 | async-start | bytes 8388608
  203.3 45.0 %copy-start.9 = (f32[66]{0:T(128)S(1)}, f32[66]{0:T(128)}, u32[]{:S(2)}) copy-start(f32[66]{0:T(128)} %and_convert_fusion) | copy-start | bytes 796
  490.0 105.6 %all-to-all-start.1 = ((f32[512,64,64]{0,1,2:T(8,128)}), f32[512,64,64]{0,1,2:T(8,128)}, u32[]{:S(2)}, u32[]{:S(2)}) async-start(f32[512,64,64]{0,1,2:T(8,128)} %bitcast.104), calls=%async_computation.1 | async-start | bytes 16777216 | tf_op jit(solution)/shard_map/all_to_all | solution.py:179
  914.3 99.0 %all-to-all-start.3 = ((f32[128,512,32]{0,2,1:T(8,128)}), f32[128,512,32]{0,2,1:T(8,128)}, u32[]{:S(2)}, u32[]{:S(2)}) async-start(f32[128,512,32]{0,2,1:T(8,128)} %copy.209), calls=%async_computation.3 | async-start | bytes 16777216 | tf_op jit(solution)/shard_map/all_to_all | solution.py:187
  1049.7 11.1 collective-permute-start.4
  1051.0 9.9 collective-permute-start.5
  1064.1 4.3 collective-permute-start.6
  1065.4 4.0 collective-permute-start.7
  1948.3 15.8 copy-start.4
  1949.8 6.4 collective-permute-start.8
  1951.3 6.4 collective-permute-start.9
  1958.8 4.3 collective-permute-start.10
  1960.1 4.0 collective-permute-start.11
  2056.7 12.0 copy-start.8
  (8 other events, 50.9 us)
where the time goes:
time: 2080 us
  blocking collectives  1060 us (51%)
  other arithmetic  354 us (17%)
  matrix products  223 us (11%)
  waiting for transfers between devices  203 us (10%)
  local copies, waits for them, and re-layouts  180 us (9%)
  starting transfers between devices  46.8 us (2%)
    all_to_all x2, blocking collectives, precondition(): lax.all_to_all(field, 'gx', split_axis=2, concat_axis=0, tiled=True)  372 us
    all_to_all x2, blocking collectives, precondition(): lax.all_to_all(hat, 'gx', split_axis=0, concat_axis=2, tiled=True)  372 us
    all_to_all x1, blocking collectives, precondition(): lax.all_to_all(lax.all_to_all(field, 'gx', split_axis=2, concat_axis=0, t...  97.9 us
    all_to_all x1, blocking collectives, precondition(): lax.all_to_all(lax.all_to_all(hat, 'gx', split_axis=0, concat_axis=2, til...  97.8 us
    mul x6, other arithmetic, smooth_axis(): 0.25 * (cut(field, 0, length - 2, axis) + 2.0 * cut(field, 1, length - 1,...  96.6 us
    all_to_all x1, waiting for transfers between devices, precondition(): lax.all_to_all(lax.all_to_all(hat, 'gx', split_axis=0, concat_axis=2, til...  94.1 us
    all_to_all x1, waiting for transfers between devices, precondition(): lax.all_to_all(lax.all_to_all(field, 'gx', split_axis=2, concat_axis=0, t...  94 us
    psum x2, blocking collectives, inner(): return lax.psum(jnp.sum(first * second), ('gx', 'gy'))  79.7 us
  transfers between devices with their start and end apart: 14, of which 9 were waited for; matrix products, arithmetic and copies ran while one was open for 0% of the time, Pallas kernels for 0%

commit v1 on v0

--- a/solution.py
+++ b/solution.py
@@ -177,7 +177,12 @@
 
     def precondition(field):
         whole = lax.all_to_all(
-            lax.all_to_all(field, "gx", split_axis=2, concat_axis=0, tiled=True),
+            jnp.concatenate(
+                lax.all_to_all(
+                    jnp.stack(jnp.split(field, lax.axis_size("gx"), axis=2)), "gx", 0, 0
+                ),
+                axis=0,
+            ),
             "gy",
             split_axis=2,
             concat_axis=1,

time: 2080 us -> 2170 us (1.043)
  local copies, waits for them, and re-layouts: 180 us -> 234 us
    reshape x0 -> x4, local copies, waits for them, and re-layouts: none -> 44.8 us  [precondition(): jnp.concatenate(lax.all_to_all(jnp.stack(jnp.split(field, lax.axis_size('...]
    another operation x0 -> x4, local copies, waits for them, and re-layouts: none -> 37.4 us  [precondition(): jnp.stack(jnp.split(field, lax.axis_size('gx'), axis=2))]
    unnamed x39 -> x41, local copies, waits for them, and re-layouts: 45.5 us -> 44.5 us
where the time goes in v1:
time: 2170 us; the launch traced here: 2160 us
  blocking collectives  1070 us (49%)
  other arithmetic  375 us (17%)
  local copies, waits for them, and re-layouts  234 us (11%)
  matrix products  223 us (10%)
  waiting for transfers between devices  203 us (9%)
  starting transfers between devices  46.8 us (2%)
    all_to_all x2, blocking collectives, precondition(): lax.all_to_all(jnp.stack(jnp.split(field, lax.axis_size('gx'), axis=2)),...  379 us
    all_to_all x2, blocking collectives, precondition(): lax.all_to_all(hat, 'gx', split_axis=0, concat_axis=2, tiled=True)  372 us
    all_to_all x1, blocking collectives, precondition(): lax.all_to_all(lax.all_to_all(hat, 'gx', split_axis=0, concat_axis=2, til...  98.1 us
    all_to_all x1, blocking collectives, precondition(): lax.all_to_all(jnp.concatenate(lax.all_to_all(jnp.stack(jnp.split(field,...  98 us
    mul x6, other arithmetic, smooth_axis(): 0.25 * (cut(field, 0, length - 2, axis) + 2.0 * cut(field, 1, length - 1,...  96.5 us
    all_to_all x1, waiting for transfers between devices, precondition(): lax.all_to_all(lax.all_to_all(hat, 'gx', split_axis=0, concat_axis=2, til...  94.1 us
    all_to_all x1, waiting for transfers between devices, precondition(): lax.all_to_all(jnp.concatenate(lax.all_to_all(jnp.stack(jnp.split(field,...  93.6 us
    psum x2, blocking collectives, inner(): return lax.psum(jnp.sum(first * second), ('gx', 'gy'))  80.1 us
  transfers between devices with their start and end apart: 14, of which 9 were waited for; matrix products, arithmetic and copies ran while one was open for 0% of the time, Pallas kernels for 0%

profile of v1, /device:TPU:0, one launch (start us, length us, event | category | flops | bytes accessed | tf_op | source)
XLA Modules:
  0.0 2159.2 jit_solution(3872489984283521950)
XLA Ops:
  47.0 53.6 %fusion.77 = (f32[132,68,256]{2,0,1:T(8,128)}, f32[132,68,256]{2,0,1:T(8,128)}, f32[132,68,256]{2,0,1:T(8,128)}, f32[132,68,256]{2,0,1:T(8,128)}) fusion(f32[132,68]{0,1:T(8,128)S(1)} %multiply_multiply_fusion, f32[134,70,256]{2,0,1:T(8,128)} %copy-done.2, f32[132,68,256]{2,0,1:T(8,128)} %slice.298), kind=kLoop, calls=%fused_computation.154 | loop fusion | flops 36765696 | bytes 82758720 | tf_op jit(solution)/shard_map/mul | solution.py:55
  100.6 29.3 %fusion.6 = (f32[130,68,256]{2,0,1:T(8,128)}, f32[130,68,256]{2,0,1:T(8,128)}) fusion(f32[132,68,256]{2,0,1:T(8,128)} %get-tuple-element.29, f32[132,68,256]{2,0,1:T(8,128)} %get-tuple-element.30), kind=kLoop, calls=%fused_computation.25 | loop fusion | flops 18104320 | bytes 72417280 | tf_op jit(solution)/shard_map/mul | solution.py:33
  149.8 29.4 %fusion.2 = (f32[130,68,256]{2,0,1:T(8,128)}, f32[130,68,256]{2,0,1:T(8,128)}) fusion(f32[132,68,256]{2,0,1:T(8,128)} %get-tuple-element.27, f32[132,68,256]{2,0,1:T(8,128)} %get-tuple-element.28), kind=kLoop, calls=%fused_computation.17 | loop fusion | flops 18104320 | bytes 72417280 | tf_op jit(solution)/shard_map/mul | solution.py:33
  202.9 55.1 %fusion.24 = (f32[130,66,256]{2,0,1:T(8,128)}, f32[130,66,256]{2,0,1:T(8,128)}, f32[130,66,256]{2,0,1:T(8,128)}, f32[130,66,256]{2,0,1:T(8,128)}) fusion(f32[130,66,256]{2,0,1:T(8,128)} %broadcast_multiply_fusion.3, f32[130,68,256]{2,0,1:T(8,128)} %get-tuple-element.54, f32[130]{0:T(256)S(1)} %and_convert_fusion.1, f32[130,68,256]{2,0,1:T(8,128)S(1)} %bitcast.99, ...), kind=kLoop, calls=%fused_computation.49 | loop fusion | flops 61501440 | bytes 140575232 | tf_op jit(solution)/shard_map/mul | solution.py:170
  258.0 26.8 %fusion.30 = (f32[130,66,256]{2,0,1:T(8,128)}, f32[130,66,256]{2,0,1:T(8,128)}) fusion(f32[130,66,256]{2,0,1:T(8,128)} %get-tuple-element.24, f32[130,66,256]{2,0,1:T(8,128)} %broadcast_multiply_fusion.2, f32[130,68,256]{2,0,1:T(8,128)} %get-tuple-element.53, f32[130,66,256]{2,0,1:T(8,128)} %get-tuple-element.23, f32[66]{0:T(128)S(1)} %copy-done.10), kind=kLoop, calls=%fused_computation.55 | loop fusion | flops 24161280 | bytes 70287624 | tf_op jit(solution)/shard_map/mul | solution.py:171
  323.6 188.9 %all_to_all.112 = f32[4,128,64,64]{1,3,2,0:T(8,128)} all-to-all(f32[4,128,64,64]{1,3,2,0:T(8,128)} %copy.190), channel_id=1, replica_groups=mesh['gx'=4,'gy'=8] {'gx'}, dimensions={0} | all-to-all | bytes 16777216 | tf_op jit(solution)/shard_map/all_to_all | solution.py:181
  547.0 93.6 %all-to-all-done.1 = f32[512,64,64]{0,1,2:T(8,128)} async-done(((f32[512,64,64]{0,1,2:T(8,128)}), f32[512,64,64]{0,1,2:T(8,128)}, u32[]{:S(2)}, u32[]{:S(2)}) %all-to-all-start.1) | async-done | bytes 8388640 | tf_op jit(solution)/shard_map/all_to_all | solution.py:179
  648.7 22.4 %fusion.66 = f32[8,512,512]{2,1,0:T(8,128)S(1)} fusion(f32[512,512,8]{0,2,1:T(8,128)S(1)} %bitcast.108, f32[512]{0:T(512)S(1)} %get-tuple-element.57, f32[512]{0:T(512)S(1)} %get-tuple-element.58), kind=kOutput, calls=%fused_computation.117 | convolution fusion | flops 12885688320 | bytes 16781312 | tf_op jit(solution)/shard_map/ki,tij->tkj/dot_general | solution.py:99
  671.0 34.1 %fusion.64 = f32[8,512,512]{2,1,0:T(8,128)S(1)} fusion(f32[8,512,512]{2,1,0:T(8,128)S(1)} %fusion.66, f32[512]{0:T(512)S(1)} %get-tuple-element.57, f32[512]{0:T(512)S(1)} %get-tuple-element.58), kind=kOutput, calls=%fused_computation.115 | convolution fusion | flops 12885688320 | bytes 16781312 | tf_op jit(solution)/shard_map/lj,tkj->tkl/dot_general | solution.py:100
  725.0 23.4 %convolution_bitcast_fusion.1 = f32[512,512,8]{0,1,2:T(8,128)} fusion(f32[8,512,512]{1,2,0:T(8,128)S(1)} %fusion.72, f32[512]{0:T(512)S(1)} %get-tuple-element.57, f32[512]{0:T(512)S(1)} %get-tuple-element.58), kind=kOutput, calls=%fused_computation.152 | convolution fusion | flops 12885688320 | bytes 16781312 | tf_op jit(solution)/shard_map/ki,tkj->tij/dot_general | solution.py:103
  758.9 184.8 %all_to_all.113 = f32[512,512,8]{1,2,0:T(8,128)S(1)} all-to-all(f32[512,512,8]{1,2,0:T(8,128)} %copy.198), channel_id=1, replica_groups=mesh['gx'=4,'gy'=8] {'gx'}, dimensions={0} | all-to-all | bytes 16777216 | tf_op jit(solution)/shard_map/all_to_all | solution.py:193
  964.2 94.1 %all-to-all-done.3 = f32[128,512,32]{0,2,1:T(8,128)} async-done(((f32[128,512,32]{0,2,1:T(8,128)}), f32[128,512,32]{0,2,1:T(8,128)}, u32[]{:S(2)}, u32[]{:S(2)}) %all-to-all-start.3) | async-done | bytes 8388640 | tf_op jit(solution)/shard_map/all_to_all | solution.py:192
  1114.3 36.8 %multiply_reduce_fusion.2 = (f32[]{:T(128)}, f32[]{:T(128)}, f32[128,64,256]{2,0,1:T(8,128)}) fusion(f32[128,64,256]{2,1,0:T(8,128)} %bitcast.103, f32[128,64,256]{2,0,1:T(8,128)} %copy-done.4, f32[128,64,256]{2,0,1:T(8,128)} %copy-done.8, f32[1,64,256]{2,0,1:T(1,128)S(1)} %copy.205, f32[1,64,256]{2,0,1:T(1,128)S(1)} %copy.207, ...), kind=kLoop, calls=%fused_computation.131 | loop fusion | flops 52428800 | bytes 67506184 | tf_op jit(solution)/shard_map/reduce_sum | solution.py:136
  1151.1 41.6 %all-reduce.5 = (f32[]{:T(128)}, f32[]{:T(128)}) all-reduce(f32[]{:T(128)} %get-tuple-element.15, f32[]{:T(128)} %get-tuple-element.14), channel_id=1, replica_groups=mesh['gx'=4,'gy'=8] {'gx','gy'}, use_global_device_ids=true, to_apply=%region_1.2 | all-reduce | flops 2 | bytes 16 | tf_op jit(solution)/shard_map/psum | solution.py:125
  1231.7 190.2 %all_to_all.114 = f32[4,128,64,64]{1,3,2,0:T(8,128)} all-to-all(f32[4,128,64,64]{1,3,2,0:T(8,128)} %copy.217), channel_id=1, replica_groups=mesh['gx'=4,'gy'=8] {'gx'}, dimensions={0} | all-to-all | bytes 16777216 | tf_op jit(solution)/shard_map/all_to_all | solution.py:181
  1444.4 98.0 %all_to_all.115 = f32[512,64,64]{0,1,2:T(8,128)S(1)} all-to-all(f32[512,64,64]{0,1,2:T(8,128)} %reshape.182), channel_id=1, replica_groups=mesh['gx'=4,'gy'=8] {'gy'}, dimensions={2} | all-to-all | bytes 16777216 | tf_op jit(solution)/shard_map/all_to_all | solution.py:179
  1547.2 22.6 %fusion.62 = f32[8,512,512]{2,1,0:T(8,128)S(1)} fusion(f32[512,512,8]{0,2,1:T(8,128)S(1)} %bitcast.109, f32[512]{0:T(512)S(1)} %get-tuple-element.57, f32[512]{0:T(512)S(1)} %get-tuple-element.58), kind=kOutput, calls=%fused_computation.113 | convolution fusion | flops 12885688320 | bytes 16781312 | tf_op jit(solution)/shard_map/ki,tij->tkj/dot_general | solution.py:99
  1569.8 34.1 %fusion.60 = f32[8,512,512]{2,1,0:T(8,128)S(1)} fusion(f32[8,512,512]{2,1,0:T(8,128)S(1)} %fusion.62, f32[512]{0:T(512)S(1)} %get-tuple-element.57, f32[512]{0:T(512)S(1)} %get-tuple-element.58), kind=kOutput, calls=%fused_computation.111 | convolution fusion | flops 12885688320 | bytes 16781312 | tf_op jit(solution)/shard_map/lj,tkj->tkl/dot_general | solution.py:100
  1623.8 23.2 %convolution_bitcast_fusion = f32[512,512,8]{0,1,2:T(8,128)} fusion(f32[8,512,512]{1,2,0:T(8,128)S(1)} %fusion.70, f32[512]{0:T(512)S(1)} %get-tuple-element.57, f32[512]{0:T(512)S(1)} %get-tuple-element.58), kind=kOutput, calls=%fused_computation.151 | convolution fusion | flops 12885688320 | bytes 16781312 | tf_op jit(solution)/shard_map/ki,tkj->tij/dot_general | solution.py:103
  1657.4 187.0 %all_to_all.116 = f32[512,512,8]{1,2,0:T(8,128)S(1)} all-to-all(f32[512,512,8]{1,2,0:T(8,128)} %copy.225), channel_id=1, replica_groups=mesh['gx'=4,'gy'=8] {'gx'}, dimensions={0} | all-to-all | bytes 16777216 | tf_op jit(solution)/shard_map/all_to_all | solution.py:193
  1859.6 98.1 %all_to_all.117 = f32[128,512,32]{0,2,1:T(8,128)S(1)} all-to-all(f32[128,512,32]{0,2,1:T(8,128)} %copy.227), channel_id=1, replica_groups=mesh['gx'=4,'gy'=8] {'gy'}, dimensions={1} | all-to-all | bytes 16777216 | tf_op jit(solution)/shard_map/all_to_all | solution.py:192
  1976.6 38.5 %psum.30 = f32[]{:T(128)} all-reduce(f32[]{:T(128)} %get-tuple-element.51), channel_id=1, replica_groups=mesh['gx'=4,'gy'=8] {'gx','gy'}, use_global_device_ids=true, to_apply=%region_5.6 | all-reduce | flops 1 | bytes 8 | tf_op jit(solution)/shard_map/psum | solution.py:125
  2046.2 20.2 multiply_reduce_fusion
  2066.4 45.2 %psum.31 = f32[]{:T(128)} all-reduce(f32[]{:T(128)} %get-tuple-element.18), channel_id=1, replica_groups=mesh['gx'=4,'gy'=8] {'gx','gy'}, use_global_device_ids=true, to_apply=%region_7.8 | all-reduce | flops 1 | bytes 8 | tf_op jit(solution)/shard_map/psum | solution.py:136
  (126 shorter events, 483.3 us)
Async XLA Ops:
  12.4 10.5 collective-permute-start
  17.3 9.7 collective-permute-start.1
  18.7 16.2 copy-start.7
  28.2 3.7 collective-permute-start.2
  29.5 5.4 collective-permute-start.3
  129.9 14.9 copy-start
  179.2 14.9 copy-start.1
  179.2 20.3 slice-start
  179.2 20.3 slice-start.1
  179.2 21.7 %slice-start.3 = ((s8[9469952]{0:T(1024)(128)(4,1)}), s8[4194304]{0:T(1024)(128)(4,1)S(1)}, s32[]{:S(2)}) async-start(s8[9469952]{0:T(1024)(128)(4,1)} %bitcast.100), calls=%async_computation.11 | async-start | bytes 8388608
  179.2 22.9 %slice-start.4 = ((s8[9469952]{0:T(1024)(128)(4,1)}), s8[4194304]{0:T(1024)(128)(4,1)S(1)}, s32[]{:S(2)}) async-start(s8[9469952]{0:T(1024)(128)(4,1)} %bitcast.100), calls=%async_computation.12 | async-start | bytes 8388608
  202.9 55.1 %copy-start.10 = (f32[66]{0:T(128)S(1)}, f32[66]{0:T(128)}, u32[]{:S(2)}) copy-start(f32[66]{0:T(128)} %and_convert_fusion) | copy-start | bytes 796
  534.9 105.6 %all-to-all-start.1 = ((f32[512,64,64]{0,1,2:T(8,128)}), f32[512,64,64]{0,1,2:T(8,128)}, u32[]{:S(2)}, u32[]{:S(2)}) async-start(f32[512,64,64]{0,1,2:T(8,128)} %reshape.181), calls=%async_computation.1 | async-start | bytes 16777216 | tf_op jit(solution)/shard_map/all_to_all | solution.py:179
  959.2 99.0 %all-to-all-start.3 = ((f32[128,512,32]{0,2,1:T(8,128)}), f32[128,512,32]{0,2,1:T(8,128)}, u32[]{:S(2)}, u32[]{:S(2)}) async-start(f32[128,512,32]{0,2,1:T(8,128)} %copy.200), calls=%async_computation.3 | async-start | bytes 16777216 | tf_op jit(solution)/shard_map/all_to_all | solution.py:192
  1094.7 11.0 collective-permute-start.4
  1096.0 9.7 collective-permute-start.5
  1109.0 4.3 collective-permute-start.6
  1110.3 4.0 collective-permute-start.7
  1859.6 102.4 %slice-start.6 = ((s8[8388608]{0:T(1024)(128)(4,1)}), s8[4194304]{0:T(1024)(128)(4,1)S(1)}, s32[]{:S(2)}) async-start(s8[8388608]{0:T(1024)(128)(4,1)} %bitcast.106), calls=%async_computation.14 | async-start | bytes 8388608
  2030.5 15.8 copy-start.5
  2031.9 6.4 collective-permute-start.8
  2033.5 6.4 collective-permute-start.9
  2040.9 4.3 collective-permute-start.10
  2042.2 4.0 collective-permute-start.11
  (9 other events, 59.7 us)
